TPU v7x, 32 devices: a whole 2x2x4 slice. The times are simulated.
32 devices in a mesh: space: 8 (over z, x), chan: 4 (over y, core).
Axes of the slice: x: 2, y: 2, z: 4, core: 2. Of those that a mesh axis runs over, the one named last changes fastest.
Arguments:
- inputs: bfloat16 [16, 256, 1024], P(None, 'chan', 'space'), may hold values from -6 to 6
- kernel_one: bfloat16 [256, 3, 3, 256], P('chan'), may hold values from -0.125 to 0.125
- kernel_two: bfloat16 [256, 3, 3, 256], P('chan'), may hold values from -0.125 to 0.125
- cotangent: bfloat16 [16, 256, 1024], P(None, 'chan', 'space'), may hold values from -6 to 6
Outputs:
- result: bfloat16 [16, 256, 1024], P(None, 'chan', 'space')
- grad_inputs: bfloat16 [16, 256, 1024], P(None, 'chan', 'space')
- grad_kernel_one: float32 [256, 3, 3, 256], P('chan')
- grad_kernel_two: float32 [256, 3, 3, 256], P('chan')
All inputs are finite; a program needn't handle non-finite values.
Results may differ from a plain program's by a relative error of at most 0.019.
Values may be sent and summed in bfloat16 or wider, within the bound.
A program may use at most 64 MiB of HBM per device.

v0:
```python
import jax
import jax.numpy as jnp
from jax import lax
from jax.sharding import PartitionSpec as P


def with_halo(block, sides, width):
    for axis, dim in sides:
        count = lax.axis_size(axis)
        forward = [(i, i + 1) for i in range(count - 1)]
        backward = [(target, source) for source, target in forward]
        low = lax.ppermute(
            lax.slice_in_dim(block, block.shape[dim] - width, None, axis=dim), axis, forward
        )
        high = lax.ppermute(lax.slice_in_dim(block, 0, width, axis=dim), axis, backward)
        block = jnp.concatenate([low, block, high], axis=dim)
    return block


def framed(values):
    wide = with_halo(values, (("space", 2),), 1)
    return jnp.pad(wide, ((1, 1), (0, 0), (0, 0)))


def valid_conv(padded, kernel):
    return lax.conv_general_dilated(
        padded[None],
        kernel,
        (1, 1),
        "VALID",
        dimension_numbers=("NHCW", "OHWI", "NHCW"),
        preferred_element_type=jnp.float32,
    )[0]


def flipped(kernel):
    return jnp.transpose(kernel[:, ::-1, ::-1], (3, 1, 2, 0))


def silu_slope(preact):
    sigmoid_part = jax.nn.sigmoid(preact)
    return sigmoid_part * (1.0 + preact * (1.0 - sigmoid_part))


def tap_products(padded, gradient):
    height, width = (gradient.shape[0], gradient.shape[2])
    pieces = []
    for row_tap in range(3):
        for col_tap in range(3):
            window = padded[row_tap : row_tap + height, :, col_tap : col_tap + width]
            pieces.append(
                jnp.einsum("hiw,how->oi", window, gradient, preferred_element_type=jnp.float32)
            )
    return jnp.stack(pieces, axis=1).reshape(gradient.shape[1], 3, 3, padded.shape[1])


def spread_out(padded):
    return lax.all_gather(padded, "chan", axis=1, tiled=True)


def backward_collect(padded, kernel):
    return lax.psum_scatter(
        valid_conv(padded, flipped(kernel)).astype(jnp.bfloat16),
        "chan",
        scatter_dimension=1,
        tiled=True,
    ).astype(jnp.float32)


def local(inputs, kernel_one, kernel_two, cotangent):
    framed_input = framed(inputs)
    all_input = spread_out(framed_input)
    pre_one = valid_conv(all_input, kernel_one)
    hidden = jax.nn.silu(pre_one).astype(jnp.bfloat16)
    all_hidden = spread_out(framed(hidden))
    pre_two = valid_conv(all_hidden, kernel_two)
    result = jax.nn.silu(pre_two).astype(jnp.bfloat16)
    grad_two = (cotangent.astype(jnp.float32) * silu_slope(pre_two)).astype(jnp.bfloat16)
    sum_two = tap_products(all_hidden, grad_two)
    grad_hidden = backward_collect(framed(grad_two), kernel_two)
    grad_one = (grad_hidden * silu_slope(pre_one)).astype(jnp.bfloat16)
    sum_one = tap_products(all_input, grad_one)
    grad_inputs = backward_collect(framed(grad_one), kernel_one).astype(jnp.bfloat16)
    sum_one, sum_two = lax.psum((sum_one, sum_two), "space")
    return (result, grad_inputs, sum_one, sum_two)


def solution(mesh):
    in_specs = (
        P(None, "chan", "space"),
        P("chan", None, None, None),
        P("chan", None, None, None),
        P(None, "chan", "space"),
    )
    out_specs = (
        P(None, "chan", "space"),
        P(None, "chan", "space"),
        P("chan", None, None, None),
        P("chan", None, None, None),
    )
    return jax.shard_map(local, mesh=mesh, in_specs=in_specs, out_specs=out_specs, check_vma=False)
```

profile of v0, /device:TPU:0, one launch (start us, length us, event | category | flops | bytes accessed | tf_op | source)
XLA Modules:
  0.0 298.1 jit_solution(694349623031645975)
XLA Ops:
  7.2 1.2 fusion.110
  8.4 4.9 %collective-permute-start = (bf16[16,64,1]{2,1,0:T(8,128)(2,1)S(1)}, bf16[16,64,1]{2,1,0:T(8,128)(2,1)S(1)}, u32[]{:S(2)}, u32[]{:S(2)}) collective-permute-start(bf16[16,64,1]{2,1,0:T(8,128)(2,1)S(1)} %get-tuple-element.22), channel_id=1, source_target_pairs={{0,4},{4,8},{8,12},{12,16},{16,20},{20,24},{24,28},{1,5},{5,9},{9,... | collective-permute-start | bytes 6152 | tf_op jit(solution)/shard_map/ppermute | solution.py:12
  13.3 1.3 collective-permute-start.1
  14.6 9.8 %collective-permute-done = bf16[16,64,1]{2,1,0:T(8,128)(2,1)S(1)} collective-permute-done((bf16[16,64,1]{2,1,0:T(8,128)(2,1)S(1)}, bf16[16,64,1]{2,1,0:T(8,128)(2,1)S(1)}, u32[]{:S(2)}, u32[]{:S(2)}) %collective-permute-start) | collective-permute-done | bytes 2080 | tf_op jit(solution)/shard_map/ppermute | solution.py:12
  24.5 2.1 select_maximum_fusion.6
  26.6 26.4 %all-gather.3.cloned.1.call-done = bf16[18,256,130]{2,1,0:T(8,128)(2,1)} async-done(((bf16[18,64,130]{2,1,0:T(8,128)(2,1)}), bf16[18,256,130]{2,1,0:T(8,128)(2,1)}) %all-gather.3.cloned.1.call-update) | async-done | bytes 1198096 | tf_op jit(solution)/shard_map/all_gather | solution.py:58
  53.0 2.8 copy.52
  57.4 2.9 fusion.21
  61.3 3.4 %collective-permute-start.2 = (bf16[16,64,1]{2,1,0:T(8,128)(2,1)S(1)}, bf16[16,64,1]{2,1,0:T(8,128)(2,1)S(1)}, u32[]{:S(2)}, u32[]{:S(2)}) collective-permute-start(bf16[16,64,1]{2,1,0:T(8,128)(2,1)S(1)} %get-tuple-element.20), channel_id=1, source_target_pairs={{0,4},{4,8},{8,12},{12,16},{16,20},{20,24},{24,28},{1,5},{5,9},{9,... | collective-permute-start | bytes 6152 | tf_op jit(solution)/shard_map/ppermute | solution.py:12
  64.7 1.3 collective-permute-start.3
  66.0 10.3 %collective-permute-done.2 = bf16[16,64,1]{2,1,0:T(8,128)(2,1)S(1)} collective-permute-done((bf16[16,64,1]{2,1,0:T(8,128)(2,1)S(1)}, bf16[16,64,1]{2,1,0:T(8,128)(2,1)S(1)}, u32[]{:S(2)}, u32[]{:S(2)}) %collective-permute-start.2) | collective-permute-done | bytes 2080 | tf_op jit(solution)/shard_map/ppermute | solution.py:12
  76.2 1.1 select_maximum_fusion.4
  77.4 25.2 %all-gather.5.cloned.1.call-done = bf16[18,256,130]{2,1,0:T(8,128)(2,1)} async-done(((bf16[18,64,130]{2,1,0:T(8,128)(2,1)}), bf16[18,256,130]{2,1,0:T(8,128)(2,1)}) %all-gather.5.cloned.1.call-update) | async-done | bytes 1198096 | tf_op jit(solution)/shard_map/all_gather | solution.py:58
  102.6 2.8 copy.53
  106.4 2.9 fusion.18
  111.6 3.4 %collective-permute-start.4 = (bf16[16,64,1]{2,1,0:T(8,128)(2,1)S(1)}, bf16[16,64,1]{2,1,0:T(8,128)(2,1)S(1)}, u32[]{:S(2)}, u32[]{:S(2)}) collective-permute-start(bf16[16,64,1]{2,1,0:T(8,128)(2,1)S(1)} %get-tuple-element.18), channel_id=1, source_target_pairs={{0,4},{4,8},{8,12},{12,16},{16,20},{20,24},{24,28},{1,5},{5,9},{9,... | collective-permute-start | bytes 6152 | tf_op jit(solution)/shard_map/ppermute | solution.py:12
  115.0 1.5 collective-permute-start.5
  116.4 10.1 %collective-permute-done.4 = bf16[16,64,1]{2,1,0:T(8,128)(2,1)S(1)} collective-permute-done((bf16[16,64,1]{2,1,0:T(8,128)(2,1)S(1)}, bf16[16,64,1]{2,1,0:T(8,128)(2,1)S(1)}, u32[]{:S(2)}, u32[]{:S(2)}) %collective-permute-start.4) | collective-permute-done | bytes 2080 | tf_op jit(solution)/shard_map/ppermute | solution.py:12
  129.1 1.7 copy.51
  130.9 1.8 fusion.33
  137.0 19.9 %reduce-scatter.3.cloned.1.call-done = bf16[16,64,128]{2,1,0:T(8,128)(2,1)} async-done(((bf16[16,256,128]{2,1,0:T(8,128)(2,1)}), bf16[16,64,128]{2,1,0:T(8,128)(2,1)}) %reduce-scatter.3.cloned.1.call-update) | async-done | bytes 262160 | tf_op jit(solution)/shard_map/reduce_scatter | solution.py:62
  157.0 1.2 fusion.92
  158.3 3.4 %collective-permute-start.6 = (bf16[16,64,1]{2,1,0:T(8,128)(2,1)S(1)}, bf16[16,64,1]{2,1,0:T(8,128)(2,1)S(1)}, u32[]{:S(2)}, u32[]{:S(2)}) collective-permute-start(bf16[16,64,1]{2,1,0:T(8,128)(2,1)S(1)} %get-tuple-element.16), channel_id=1, source_target_pairs={{0,4},{4,8},{8,12},{12,16},{16,20},{20,24},{24,28},{1,5},{5,9},{9,... | collective-permute-start | bytes 6152 | tf_op jit(solution)/shard_map/ppermute | solution.py:12
  161.7 1.3 collective-permute-start.7
  163.0 2.1 fusion.25
  165.1 7.7 %collective-permute-done.6 = bf16[16,64,1]{2,1,0:T(8,128)(2,1)S(1)} collective-permute-done((bf16[16,64,1]{2,1,0:T(8,128)(2,1)S(1)}, bf16[16,64,1]{2,1,0:T(8,128)(2,1)S(1)}, u32[]{:S(2)}, u32[]{:S(2)}) %collective-permute-start.6) | collective-permute-done | bytes 2080 | tf_op jit(solution)/shard_map/ppermute | solution.py:12
  176.1 2.3 copy.47
  178.7 1.8 fusion.42
  185.6 18.9 %reduce-scatter.5.cloned.1.call-done = bf16[16,64,128]{2,0,1:T(8,128)(2,1)} async-done(((bf16[16,256,128]{2,0,1:T(8,128)(2,1)}), bf16[16,64,128]{2,0,1:T(8,128)(2,1)}) %reduce-scatter.5.cloned.1.call-update) | async-done | bytes 262160 | tf_op jit(solution)/shard_map/reduce_scatter | solution.py:62
  204.5 1.7 copy.48
  206.2 82.5 %all-reduce.7.cloned.1.call-done = (f32[64,3,3,256]{3,0,2,1:T(8,128)}, f32[64,3,3,256]{3,0,2,1:T(8,128)}) async-done(((f32[64,3,3,256]{3,0,2,1:T(8,128)}, f32[64,3,3,256]{3,0,2,1:T(8,128)}), (f32[64,3,3,256]{3,0,2,1:T(8,128)}, f32[64,3,3,256]{3,0,2,1:T(8,128)})) %all-reduce.7.cloned.1.call-update) | async-done | bytes 1179664 | tf_op jit(solution)/shard_map/psum | solution.py:84
  288.7 2.0 copy.74
  (93 shorter events, 22.1 us)
Async XLA Ops:
  7.2 99.2 %copy-start = (bf16[64,3,3,256]{3,0,2,1:T(8,128)(2,1)S(1)}, bf16[64,3,3,256]{3,0,2,1:T(8,128)(2,1)}, u32[]{:S(2)}) copy-start(bf16[64,3,3,256]{3,0,2,1:T(8,128)(2,1)} %param.6) | copy-start | bytes 884740
  7.2 45.8 %all-gather.3.cloned.1.call-start = ((), (), s32[]{:S(2)}) async-start(), calls=%async_computation.2 | async-start | bytes 2949120 | tf_op jit(solution)/shard_map/all_gather | solution.py:58
  8.4 16.0 %collective-permute-start = (bf16[16,64,1]{2,1,0:T(8,128)(2,1)S(1)}, bf16[16,64,1]{2,1,0:T(8,128)(2,1)S(1)}, u32[]{:S(2)}, u32[]{:S(2)}) collective-permute-start(bf16[16,64,1]{2,1,0:T(8,128)(2,1)S(1)} %get-tuple-element.22), channel_id=1, source_target_pairs={{0,4},{4,8},{8,12},{12,16},{16,20},{20,24},{24,28},{1,5},{5,9},{9,... | collective-permute-start | bytes 6152 | tf_op jit(solution)/shard_map/ppermute | solution.py:12
  13.3 11.2 %collective-permute-start.1 = (bf16[16,64,1]{2,1,0:T(8,128)(2,1)S(1)}, bf16[16,64,1]{2,1,0:T(8,128)(2,1)S(1)}, u32[]{:S(2)}, u32[]{:S(2)}) collective-permute-start(bf16[16,64,1]{2,1,0:T(8,128)(2,1)S(1)} %get-tuple-element.23), channel_id=1, source_target_pairs={{4,0},{8,4},{12,8},{16,12},{20,16},{24,20},{28,24},{5,1},{9,5},{13... | collective-permute-start | bytes 6152 | tf_op jit(solution)/shard_map/ppermute | solution.py:15
  26.6 76.1 %all-gather.5.cloned.1.call-start = ((), (), s32[]{:S(2)}) async-start(), calls=%async_computation.3 | async-start | bytes 2949120 | tf_op jit(solution)/shard_map/all_gather | solution.py:58
  56.4 1.0 copy-start.10
  56.4 1.0 copy-start.12
  61.0 16.4 %copy-start.1 = (f32[16,1,128,64]{2,3,0,1:T(8,128)}, f32[16,1,128,64]{2,3,0,1:T(8,128)S(1)}, u32[]{:S(2)}) copy-start(f32[16,1,128,64]{2,3,0,1:T(8,128)S(1)} %copy.49) | copy-start | bytes 1572868
  61.3 15.0 %collective-permute-start.2 = (bf16[16,64,1]{2,1,0:T(8,128)(2,1)S(1)}, bf16[16,64,1]{2,1,0:T(8,128)(2,1)S(1)}, u32[]{:S(2)}, u32[]{:S(2)}) collective-permute-start(bf16[16,64,1]{2,1,0:T(8,128)(2,1)S(1)} %get-tuple-element.20), channel_id=1, source_target_pairs={{0,4},{4,8},{8,12},{12,16},{16,20},{20,24},{24,28},{1,5},{5,9},{9,... | collective-permute-start | bytes 6152 | tf_op jit(solution)/shard_map/ppermute | solution.py:12
  64.7 11.6 %collective-permute-start.3 = (bf16[16,64,1]{2,1,0:T(8,128)(2,1)S(1)}, bf16[16,64,1]{2,1,0:T(8,128)(2,1)S(1)}, u32[]{:S(2)}, u32[]{:S(2)}) collective-permute-start(bf16[16,64,1]{2,1,0:T(8,128)(2,1)S(1)} %get-tuple-element.21), channel_id=1, source_target_pairs={{4,0},{8,4},{12,8},{16,12},{20,16},{24,20},{28,24},{5,1},{9,5},{13... | collective-permute-start | bytes 6152 | tf_op jit(solution)/shard_map/ppermute | solution.py:15
  77.4 79.6 %reduce-scatter.3.cloned.1.call-start = ((), (), s32[]{:S(2)}) async-start(), calls=%async_computation.4 | async-start | bytes 1310720 | tf_op jit(solution)/shard_map/reduce_scatter | solution.py:62
  109.5 1.0 copy-start.9
  111.6 14.9 %collective-permute-start.4 = (bf16[16,64,1]{2,1,0:T(8,128)(2,1)S(1)}, bf16[16,64,1]{2,1,0:T(8,128)(2,1)S(1)}, u32[]{:S(2)}, u32[]{:S(2)}) collective-permute-start(bf16[16,64,1]{2,1,0:T(8,128)(2,1)S(1)} %get-tuple-element.18), channel_id=1, source_target_pairs={{0,4},{4,8},{8,12},{12,16},{16,20},{20,24},{24,28},{1,5},{5,9},{9,... | collective-permute-start | bytes 6152 | tf_op jit(solution)/shard_map/ppermute | solution.py:12
  115.0 11.6 %collective-permute-start.5 = (bf16[16,64,1]{2,1,0:T(8,128)(2,1)S(1)}, bf16[16,64,1]{2,1,0:T(8,128)(2,1)S(1)}, u32[]{:S(2)}, u32[]{:S(2)}) collective-permute-start(bf16[16,64,1]{2,1,0:T(8,128)(2,1)S(1)} %get-tuple-element.19), channel_id=1, source_target_pairs={{4,0},{8,4},{12,8},{16,12},{20,16},{24,20},{28,24},{5,1},{9,5},{13... | collective-permute-start | bytes 6152 | tf_op jit(solution)/shard_map/ppermute | solution.py:15
  130.8 2.0 copy-start.4
  130.9 73.6 %reduce-scatter.5.cloned.1.call-start = ((), (), s32[]{:S(2)}) async-start(), calls=%async_computation.5 | async-start | bytes 1310720 | tf_op jit(solution)/shard_map/reduce_scatter | solution.py:62
  134.4 1.7 copy-start.5
  136.0 20.9 %copy-start.2 = (f32[16,1,128,64]{2,3,0,1:T(8,128)S(1)}, f32[16,1,128,64]{2,3,0,1:T(8,128)}, u32[]{:S(2)}) copy-start(f32[16,1,128,64]{2,3,0,1:T(8,128)} %copy-done.1) | copy-start | bytes 1572868
  158.3 14.6 %collective-permute-start.6 = (bf16[16,64,1]{2,1,0:T(8,128)(2,1)S(1)}, bf16[16,64,1]{2,1,0:T(8,128)(2,1)S(1)}, u32[]{:S(2)}, u32[]{:S(2)}) collective-permute-start(bf16[16,64,1]{2,1,0:T(8,128)(2,1)S(1)} %get-tuple-element.16), channel_id=1, source_target_pairs={{0,4},{4,8},{8,12},{12,16},{16,20},{20,24},{24,28},{1,5},{5,9},{9,... | collective-permute-start | bytes 6152 | tf_op jit(solution)/shard_map/ppermute | solution.py:12
  161.7 11.2 %collective-permute-start.7 = (bf16[16,64,1]{2,1,0:T(8,128)(2,1)S(1)}, bf16[16,64,1]{2,1,0:T(8,128)(2,1)S(1)}, u32[]{:S(2)}, u32[]{:S(2)}) collective-permute-start(bf16[16,64,1]{2,1,0:T(8,128)(2,1)S(1)} %get-tuple-element.17), channel_id=1, source_target_pairs={{4,0},{8,4},{12,8},{16,12},{20,16},{24,20},{28,24},{5,1},{9,5},{13... | collective-permute-start | bytes 6152 | tf_op jit(solution)/shard_map/ppermute | solution.py:15
  165.1 8.6 %copy-start.7 = (f32[64,9,256]{2,0,1:T(8,128)}, f32[64,9,256]{2,0,1:T(8,128)S(1)}, u32[]{:S(2)}) copy-start(f32[64,9,256]{2,0,1:T(8,128)S(1)} %fusion.25) | copy-start | bytes 1769476
  173.7 1.0 copy-start.11
  178.4 2.1 copy-start.3
  178.4 110.3 %all-reduce.7.cloned.1.call-start = ((), (), s32[]{:S(2)}) async-start(), calls=%async_computation.6 | async-start | bytes 2359296 | tf_op jit(solution)/shard_map/psum | solution.py:84
  184.8 0.8 copy-start.8
  288.7 2.0 copy-start.6
Sparse Core Ops, SparseCore 0:
  26.7 26.2 all-gather.2
  77.5 25.0 all-gather.4
  131.0 25.9 reduce-scatter.2
  178.6 25.8 reduce-scatter.4
  208.4 80.2 all-reduce.6
where the time goes:
time: 299 us; the launch traced here: 298 us
  waiting for transfers between devices  211 us (71%)
  local copies, waits for them, and re-layouts  24.5 us (8%)
  matrix products  21.5 us (7%)
  starting transfers between devices  20.8 us (7%)
  between operations  14.3 us (5%)
  other arithmetic  6.14 us (2%)
    psum x1, waiting for transfers between devices, local(): sum_one, sum_two = lax.psum((sum_one, sum_two), 'space')  82.5 us
    all_gather x2, waiting for transfers between devices, spread_out(): return lax.all_gather(padded, 'chan', axis=1, tiled=True)  51.6 us
    reduce_scatter x2, waiting for transfers between devices, backward_collect(): lax.psum_scatter(valid_conv(padded, flipped(kernel)).astype(jnp.bfloat16)...  38.8 us
    ppermute x4, waiting for transfers between devices, with_halo(): lax.ppermute(lax.slice_in_dim(block, block.shape[dim] - width, None, axis...  37.9 us
    unnamed x36, local copies, waits for them, and re-layouts  16.6 us
    ppermute x4, starting transfers between devices, with_halo(): lax.ppermute(lax.slice_in_dim(block, block.shape[dim] - width, None, axis...  15 us
    dot_general x18, matrix products, tap_products(): jnp.einsum('hiw,how->oi', window, gradient, preferred_element_type=jnp.fl...  13.6 us
    conv_general_dilated x4, matrix products, valid_conv(): lax.conv_general_dilated(padded[None], kernel, (1, 1), 'VALID', dimension...  7.9 us
  transfers between devices with their start and end apart: 13, of which 9 were waited for; matrix products, arithmetic and copies ran while one was open for 5% of the time, Pallas kernels for 0%

commit v1 on v0

--- a/solution.py
+++ b/solution.py
@@ -2,6 +2,18 @@
 import jax.numpy as jnp
 from jax import lax
 from jax.sharding import PartitionSpec as P
+
+
+def doubled_up(array, axis, dim):
+    ways, here = (lax.axis_size(axis), lax.axis_index(axis))
+    grown, reach = (array, 1)
+    while reach < ways:
+        theirs = lax.ppermute(grown, axis, [(d, d ^ reach) for d in range(ways)])
+        mine_first = jnp.concatenate([grown, theirs], axis=dim)
+        theirs_first = jnp.concatenate([theirs, grown], axis=dim)
+        grown = jnp.where(here & reach == 0, mine_first, theirs_first)
+        reach = 2 * reach
+    return grown
 
 
 def with_halo(block, sides, width):
@@ -55,7 +67,7 @@
 
 
 def spread_out(padded):
-    return lax.all_gather(padded, "chan", axis=1, tiled=True)
+    return doubled_up(padded, "chan", 1)
 
 
 def backward_collect(padded, kernel):

time: 299 us -> 320 us (1.070)
  local copies, waits for them, and re-layouts: 24.5 us -> 49.9 us
  waiting for transfers between devices: 211 us -> 189 us
  other arithmetic: 6.14 us -> 15.1 us
  starting transfers between devices: 20.8 us -> 29.1 us
    all_gather x2 -> x0, waiting for transfers between devices: 51.6 us -> none  [spread_out(): return lax.all_gather(padded, 'chan', axis=1, tiled=True)]
    ppermute x0 -> x4, waiting for transfers between devices: none -> 33.6 us  [doubled_up(): theirs = lax.ppermute(grown, axis, [(d, d ^ reach) for d in range(ways)])]
    ppermute x4, waiting for transfers between devices: 37.9 us -> 22.8 us  [with_halo(): lax.ppermute(lax.slice_in_dim(block, block.shape[dim] - width, None, axis...]
    ppermute x4, waiting for transfers between devices: 0.01 us -> 11.9 us  [with_halo(): lax.ppermute(lax.slice_in_dim(block, 0, width, axis=dim), axis, backward)]
    select_n x0 -> x6, other arithmetic: none -> 8.58 us  [doubled_up(): grown = jnp.where(here & reach == 0, mine_first, theirs_first)]
    conv_general_dilated x16, local copies, waits for them, and re-layouts: 2.86 us -> 11.1 us  [valid_conv(): lax.conv_general_dilated(padded[None], kernel, (1, 1), 'VALID', dimension...]
    select_n x0 -> x4, local copies, waits for them, and re-layouts: none -> 6.88 us  [doubled_up(): grown = jnp.where(here & reach == 0, mine_first, theirs_first)]
    unnamed x36 -> x32, local copies, waits for them, and re-layouts: 16.6 us -> 22.5 us
  transfers between devices with their start and end apart: 13 -> 15, of which waited for: 9 -> 15; matrix products, arithmetic and copies ran while one was open for 5% -> 6% of each run, Pallas kernels for 0% -> 0%
where the time goes in v1:
time: 320 us; the launch traced here: 319 us
  waiting for transfers between devices  189 us (59%)
  local copies, waits for them, and re-layouts  49.9 us (16%)
  starting transfers between devices  29.1 us (9%)
  matrix products  21.7 us (7%)
  other arithmetic  15.1 us (5%)
  between operations  14.3 us (4%)
    psum x1, waiting for transfers between devices, local(): sum_one, sum_two = lax.psum((sum_one, sum_two), 'space')  82.7 us
    reduce_scatter x2, waiting for transfers between devices, backward_collect(): lax.psum_scatter(valid_conv(padded, flipped(kernel)).astype(jnp.bfloat16)...  37.6 us
    ppermute x4, waiting for transfers between devices, doubled_up(): theirs = lax.ppermute(grown, axis, [(d, d ^ reach) for d in range(ways)])  33.6 us
    ppermute x4, waiting for transfers between devices, with_halo(): lax.ppermute(lax.slice_in_dim(block, block.shape[dim] - width, None, axis...  22.8 us
    unnamed x32, local copies, waits for them, and re-layouts  22.5 us
    ppermute x4, starting transfers between devices, with_halo(): lax.ppermute(lax.slice_in_dim(block, block.shape[dim] - width, None, axis...  20.3 us
    dot_general x18, matrix products, tap_products(): jnp.einsum('hiw,how->oi', window, gradient, preferred_element_type=jnp.fl...  13.8 us
    ppermute x4, waiting for transfers between devices, with_halo(): lax.ppermute(lax.slice_in_dim(block, 0, width, axis=dim), axis, backward)  11.9 us
  transfers between devices with their start and end apart: 15, of which 15 were waited for; matrix products, arithmetic and copies ran while one was open for 6% of the time, Pallas kernels for 0%

profile of v1, /device:TPU:0, one launch (start us, length us, event | category | flops | bytes accessed | tf_op | source)
XLA Modules:
  0.0 318.8 jit_solution(2754527064047366904)
XLA Ops:
  9.7 5.5 %collective-permute-start = (bf16[16,64,1]{2,1,0:T(8,128)(2,1)S(1)}, bf16[16,64,1]{2,1,0:T(8,128)(2,1)S(1)}, u32[]{:S(2)}, u32[]{:S(2)}) collective-permute-start(bf16[16,64,1]{2,1,0:T(8,128)(2,1)S(1)} %get-tuple-element.22), channel_id=1, source_target_pairs={{0,4},{4,8},{8,12},{12,16},{16,20},{20,24},{24,28},{1,5},{5,9},{9,... | collective-permute-start | bytes 6152 | tf_op jit(solution)/shard_map/ppermute | solution.py:24
  15.2 4.3 %collective-permute-done.1 = bf16[16,64,1]{2,1,0:T(8,128)(2,1)S(1)} collective-permute-done((bf16[16,64,1]{2,1,0:T(8,128)(2,1)S(1)}, bf16[16,64,1]{2,1,0:T(8,128)(2,1)S(1)}, u32[]{:S(2)}, u32[]{:S(2)}) %collective-permute-start.1) | collective-permute-done | bytes 2080 | tf_op jit(solution)/shard_map/ppermute | solution.py:27
  19.6 5.8 %collective-permute-done = bf16[16,64,1]{2,1,0:T(8,128)(2,1)S(1)} collective-permute-done((bf16[16,64,1]{2,1,0:T(8,128)(2,1)S(1)}, bf16[16,64,1]{2,1,0:T(8,128)(2,1)S(1)}, u32[]{:S(2)}, u32[]{:S(2)}) %collective-permute-start) | collective-permute-done | bytes 2080 | tf_op jit(solution)/shard_map/ppermute | solution.py:24
  31.4 14.6 %collective-permute-done.3 = bf16[18,128,130]{1,2,0:T(8,128)(2,1)S(1)} collective-permute-done((bf16[18,128,130]{1,2,0:T(8,128)(2,1)S(1)}, bf16[18,128,130]{1,2,0:T(8,128)(2,1)S(1)}, u32[]{:S(2)}, u32[]{:S(2)}) %collective-permute-start.3) | collective-permute-done | bytes 599072 | tf_op jit(solution)/shard_map/ppermute | solution.py:11
  48.4 3.9 %copy.60 = bf16[18,256,1,130]{1,3,0,2:T(8,128)(2,1)} copy(bf16[18,256,1,130]{3,1,0,2:T(8,128)(2,1)} %fusion.2) | data formatting | bytes 2396160
  52.3 2.4 pad.17.clone
  54.8 2.3 reshape.226
  58.0 2.9 fusion.23
  63.2 5.2 %collective-permute-start.4 = (bf16[16,64,1]{2,1,0:T(8,128)(2,1)S(1)}, bf16[16,64,1]{2,1,0:T(8,128)(2,1)S(1)}, u32[]{:S(2)}, u32[]{:S(2)}) collective-permute-start(bf16[16,64,1]{2,1,0:T(8,128)(2,1)S(1)} %get-tuple-element.20), channel_id=1, source_target_pairs={{0,4},{4,8},{8,12},{12,16},{16,20},{20,24},{24,28},{1,5},{5,9},{9,... | collective-permute-start | bytes 6152 | tf_op jit(solution)/shard_map/ppermute | solution.py:24
  68.4 3.6 %collective-permute-done.5 = bf16[16,64,1]{2,1,0:T(8,128)(2,1)S(1)} collective-permute-done((bf16[16,64,1]{2,1,0:T(8,128)(2,1)S(1)}, bf16[16,64,1]{2,1,0:T(8,128)(2,1)S(1)}, u32[]{:S(2)}, u32[]{:S(2)}) %collective-permute-start.5) | collective-permute-done | bytes 2080 | tf_op jit(solution)/shard_map/ppermute | solution.py:27
  72.1 5.8 %collective-permute-done.4 = bf16[16,64,1]{2,1,0:T(8,128)(2,1)S(1)} collective-permute-done((bf16[16,64,1]{2,1,0:T(8,128)(2,1)S(1)}, bf16[16,64,1]{2,1,0:T(8,128)(2,1)S(1)}, u32[]{:S(2)}, u32[]{:S(2)}) %collective-permute-start.4) | collective-permute-done | bytes 2080 | tf_op jit(solution)/shard_map/ppermute | solution.py:24
  78.3 2.0 collective-permute-done.6
  83.5 15.0 %collective-permute-done.7 = bf16[18,128,130]{1,2,0:T(8,128)(2,1)} collective-permute-done((bf16[18,128,130]{1,2,0:T(8,128)(2,1)}, bf16[18,128,130]{1,2,0:T(8,128)(2,1)}, u32[]{:S(2)}, u32[]{:S(2)}) %collective-permute-start.7) | collective-permute-done | bytes 599072 | tf_op jit(solution)/shard_map/ppermute | solution.py:11
  98.5 2.3 copy.36
  100.8 3.3 %fusion.3 = bf16[18,256,1,130]{3,1,0,2:T(8,128)(2,1)} fusion(bf16[1,18,128,130]{3,2,1,0:T(8,128)(2,1)} %bitcast.224, bf16[1,18,128,130]{3,2,1,0:T(8,128)(2,1)S(1)} %bitcast.222, pred[]{:T(512)S(6)} %eq.8), kind=kLoop, calls=%fused_computation.6 | loop fusion | flops 5391360 | bytes 2396161 | tf_op jit(solution)/shard_map/jit(_where)/select_n | solution.py:14
  104.1 3.9 %copy.61 = bf16[18,256,1,130]{1,3,0,2:T(8,128)(2,1)} copy(bf16[18,256,1,130]{3,1,0,2:T(8,128)(2,1)} %fusion.3) | data formatting | bytes 2396160
  108.0 2.4 pad.19.clone
  110.4 3.3 %reshape.233 = bf16[18,256,1,8,17]{1,4,3,0,2:T(8,128)(2,1)} reshape(bf16[18,256,1,136]{1,3,0,2:T(8,128)(2,1)} %pad.19.clone) | data formatting | bytes 2506752 | tf_op jit(solution)/shard_map/conv_general_dilated | solution.py:38
  115.5 2.9 fusion.20
  119.6 2.4 copy.58
  122.1 2.2 fusion.86
  125.7 5.0 %collective-permute-start.8 = (bf16[16,64,1]{2,1,0:T(8,128)(2,1)S(1)}, bf16[16,64,1]{2,1,0:T(8,128)(2,1)S(1)}, u32[]{:S(2)}, u32[]{:S(2)}) collective-permute-start(bf16[16,64,1]{2,1,0:T(8,128)(2,1)S(1)} %get-tuple-element.18), channel_id=1, source_target_pairs={{0,4},{4,8},{8,12},{12,16},{16,20},{20,24},{24,28},{1,5},{5,9},{9,... | collective-permute-start | bytes 6152 | tf_op jit(solution)/shard_map/ppermute | solution.py:24
  134.5 5.8 %collective-permute-done.8 = bf16[16,64,1]{2,1,0:T(8,128)(2,1)S(1)} collective-permute-done((bf16[16,64,1]{2,1,0:T(8,128)(2,1)S(1)}, bf16[16,64,1]{2,1,0:T(8,128)(2,1)S(1)}, u32[]{:S(2)}, u32[]{:S(2)}) %collective-permute-start.8) | collective-permute-done | bytes 2080 | tf_op jit(solution)/shard_map/ppermute | solution.py:24
  147.7 2.7 copy.59
  155.6 21.1 %reduce-scatter.3.cloned.1.call-done = bf16[16,64,128]{2,1,0:T(8,128)(2,1)} async-done(((bf16[16,256,128]{2,1,0:T(8,128)(2,1)}), bf16[16,64,128]{2,1,0:T(8,128)(2,1)}) %reduce-scatter.3.cloned.1.call-update) | async-done | bytes 262160 | tf_op jit(solution)/shard_map/reduce_scatter | solution.py:74
  179.3 4.6 %collective-permute-start.10 = (bf16[16,64,1]{2,1,0:T(8,128)(2,1)S(1)}, bf16[16,64,1]{2,1,0:T(8,128)(2,1)S(1)}, u32[]{:S(2)}, u32[]{:S(2)}) collective-permute-start(bf16[16,64,1]{2,1,0:T(8,128)(2,1)S(1)} %get-tuple-element.16), channel_id=1, source_target_pairs={{0,4},{4,8},{8,12},{12,16},{16,20},{20,24},{24,28},{1,5},{5,9},{9,... | collective-permute-start | bytes 6152 | tf_op jit(solution)/shard_map/ppermute | solution.py:24
  183.8 2.1 fusion.27
  187.9 5.5 %collective-permute-done.10 = bf16[16,64,1]{2,1,0:T(8,128)(2,1)S(1)} collective-permute-done((bf16[16,64,1]{2,1,0:T(8,128)(2,1)S(1)}, bf16[16,64,1]{2,1,0:T(8,128)(2,1)S(1)}, u32[]{:S(2)}, u32[]{:S(2)}) %collective-permute-start.10) | collective-permute-done | bytes 2080 | tf_op jit(solution)/shard_map/ppermute | solution.py:24
  196.5 2.4 copy.51
  200.8 2.1 fusion.43
  207.4 16.6 %reduce-scatter.5.cloned.1.call-done = bf16[16,64,128]{2,0,1:T(8,128)(2,1)} async-done(((bf16[16,256,128]{2,0,1:T(8,128)(2,1)}), bf16[16,64,128]{2,0,1:T(8,128)(2,1)}) %reduce-scatter.5.cloned.1.call-update) | async-done | bytes 262160 | tf_op jit(solution)/shard_map/reduce_scatter | solution.py:74
  225.7 82.7 %all-reduce.7.cloned.1.call-done = (f32[64,3,3,256]{3,0,2,1:T(8,128)}, f32[64,3,3,256]{3,0,2,1:T(8,128)}) async-done(((f32[64,3,3,256]{3,0,2,1:T(8,128)}, f32[64,3,3,256]{3,0,2,1:T(8,128)}), (f32[64,3,3,256]{3,0,2,1:T(8,128)}, f32[64,3,3,256]{3,0,2,1:T(8,128)})) %all-reduce.7.cloned.1.call-update) | async-done | bytes 1179664 | tf_op jit(solution)/shard_map/psum | solution.py:96
  (101 shorter events, 58.1 us)
Async XLA Ops:
  7.2 108.3 %copy-start = (bf16[64,3,3,256]{3,0,2,1:T(8,128)(2,1)S(1)}, bf16[64,3,3,256]{3,0,2,1:T(8,128)(2,1)}, u32[]{:S(2)}) copy-start(bf16[64,3,3,256]{3,0,2,1:T(8,128)(2,1)} %param.6) | copy-start | bytes 884740
  7.2 169.5 %reduce-scatter.3.cloned.1.call-start = ((), (), s32[]{:S(2)}) async-start(), calls=%async_computation.2 | async-start | bytes 1310720 | tf_op jit(solution)/shard_map/reduce_scatter | solution.py:74
  8.4 11.1 %collective-permute-start.1 = (bf16[16,64,1]{2,1,0:T(8,128)(2,1)S(1)}, bf16[16,64,1]{2,1,0:T(8,128)(2,1)S(1)}, u32[]{:S(2)}, u32[]{:S(2)}) collective-permute-start(bf16[16,64,1]{2,1,0:T(8,128)(2,1)S(1)} %get-tuple-element.23), channel_id=1, source_target_pairs={{4,0},{8,4},{12,8},{16,12},{20,16},{24,20},{28,24},{5,1},{9,5},{13... | collective-permute-start | bytes 6152 | tf_op jit(solution)/shard_map/ppermute | solution.py:27
  9.7 15.6 %collective-permute-start = (bf16[16,64,1]{2,1,0:T(8,128)(2,1)S(1)}, bf16[16,64,1]{2,1,0:T(8,128)(2,1)S(1)}, u32[]{:S(2)}, u32[]{:S(2)}) collective-permute-start(bf16[16,64,1]{2,1,0:T(8,128)(2,1)S(1)} %get-tuple-element.22), channel_id=1, source_target_pairs={{0,4},{4,8},{8,12},{12,16},{16,20},{20,24},{24,28},{1,5},{5,9},{9,... | collective-permute-start | bytes 6152 | tf_op jit(solution)/shard_map/ppermute | solution.py:24
  26.6 2.1 collective-permute-start.2
  29.8 16.2 %collective-permute-start.3 = (bf16[18,128,130]{1,2,0:T(8,128)(2,1)S(1)}, bf16[18,128,130]{1,2,0:T(8,128)(2,1)S(1)}, u32[]{:S(2)}, u32[]{:S(2)}) collective-permute-start(bf16[18,128,130]{1,2,0:T(8,128)(2,1)S(1)} %copy.28), channel_id=1, source_target_pairs={{0,2},{1,3},{2,0},{3,1},{4,6},{5,7},{6,4},{7,5},{8,10},{9,11},{10,... | collective-permute-start | bytes 1797128 | tf_op jit(solution)/shard_map/ppermute | solution.py:11
  46.6 1.8 copy-start.1
  57.1 1.0 copy-start.8
  57.1 1.0 copy-start.10
  61.9 10.2 %collective-permute-start.5 = (bf16[16,64,1]{2,1,0:T(8,128)(2,1)S(1)}, bf16[16,64,1]{2,1,0:T(8,128)(2,1)S(1)}, u32[]{:S(2)}, u32[]{:S(2)}) collective-permute-start(bf16[16,64,1]{2,1,0:T(8,128)(2,1)S(1)} %get-tuple-element.21), channel_id=1, source_target_pairs={{4,0},{8,4},{12,8},{16,12},{20,16},{24,20},{28,24},{5,1},{9,5},{13... | collective-permute-start | bytes 6152 | tf_op jit(solution)/shard_map/ppermute | solution.py:27
  63.2 14.6 %collective-permute-start.4 = (bf16[16,64,1]{2,1,0:T(8,128)(2,1)S(1)}, bf16[16,64,1]{2,1,0:T(8,128)(2,1)S(1)}, u32[]{:S(2)}, u32[]{:S(2)}) collective-permute-start(bf16[16,64,1]{2,1,0:T(8,128)(2,1)S(1)} %get-tuple-element.20), channel_id=1, source_target_pairs={{0,4},{4,8},{8,12},{12,16},{16,20},{20,24},{24,28},{1,5},{5,9},{9,... | collective-permute-start | bytes 6152 | tf_op jit(solution)/shard_map/ppermute | solution.py:24
  78.2 2.1 collective-permute-start.6
  82.0 16.5 %collective-permute-start.7 = (bf16[18,128,130]{1,2,0:T(8,128)(2,1)}, bf16[18,128,130]{1,2,0:T(8,128)(2,1)}, u32[]{:S(2)}, u32[]{:S(2)}) collective-permute-start(bf16[18,128,130]{1,2,0:T(8,128)(2,1)} %copy.35), channel_id=1, source_target_pairs={{0,2},{1,3},{2,0},{3,1},{4,6},{5,7},{6,4},{7,5},{8,10},{9,11},{10,... | collective-permute-start | bytes 1797128 | tf_op jit(solution)/shard_map/ppermute | solution.py:11
  122.1 8.7 %copy-start.2 = (bf16[18,128,130]{2,1,0:T(8,128)(2,1)S(1)}, bf16[18,128,130]{2,1,0:T(8,128)(2,1)}, u32[]{:S(2)}) copy-start(bf16[18,128,130]{2,1,0:T(8,128)(2,1)} %copy-done.1) | copy-start | bytes 1797124
  124.4 10.2 %collective-permute-start.9 = (bf16[16,64,1]{2,1,0:T(8,128)(2,1)S(1)}, bf16[16,64,1]{2,1,0:T(8,128)(2,1)S(1)}, u32[]{:S(2)}, u32[]{:S(2)}) collective-permute-start(bf16[16,64,1]{2,1,0:T(8,128)(2,1)S(1)} %get-tuple-element.19), channel_id=1, source_target_pairs={{4,0},{8,4},{12,8},{16,12},{20,16},{24,20},{28,24},{5,1},{9,5},{13... | collective-permute-start | bytes 6152 | tf_op jit(solution)/shard_map/ppermute | solution.py:27
  125.7 14.6 %collective-permute-start.8 = (bf16[16,64,1]{2,1,0:T(8,128)(2,1)S(1)}, bf16[16,64,1]{2,1,0:T(8,128)(2,1)S(1)}, u32[]{:S(2)}, u32[]{:S(2)}) collective-permute-start(bf16[16,64,1]{2,1,0:T(8,128)(2,1)S(1)} %get-tuple-element.18), channel_id=1, source_target_pairs={{0,4},{4,8},{8,12},{12,16},{16,20},{20,24},{24,28},{1,5},{5,9},{9,... | collective-permute-start | bytes 6152 | tf_op jit(solution)/shard_map/ppermute | solution.py:24
  146.7 4.0 %copy-start.3 = (bf16[18,128,130]{2,1,0:T(8,128)(2,1)S(1)}, bf16[18,128,130]{2,1,0:T(8,128)(2,1)}, u32[]{:S(2)}) copy-start(bf16[18,128,130]{2,1,0:T(8,128)(2,1)} %copy.36) | copy-start | bytes 1797124
  150.4 73.6 %reduce-scatter.5.cloned.1.call-start = ((), (), s32[]{:S(2)}) async-start(), calls=%async_computation.3 | async-start | bytes 1310720 | tf_op jit(solution)/shard_map/reduce_scatter | solution.py:74
  151.4 3.6 %copy-start.5 = (bf16[18,256,130]{2,1,0:T(8,128)(2,1)}, bf16[18,256,130]{2,1,0:T(8,128)(2,1)S(1)}, u32[]{:S(2)}) copy-start(bf16[18,256,130]{2,1,0:T(8,128)(2,1)S(1)} %maximum_select_fusion.3) | copy-start | bytes 3594244
  178.0 9.9 %collective-permute-start.11 = (bf16[16,64,1]{2,1,0:T(8,128)(2,1)S(1)}, bf16[16,64,1]{2,1,0:T(8,128)(2,1)S(1)}, u32[]{:S(2)}, u32[]{:S(2)}) collective-permute-start(bf16[16,64,1]{2,1,0:T(8,128)(2,1)S(1)} %get-tuple-element.17), channel_id=1, source_target_pairs={{4,0},{8,4},{12,8},{16,12},{20,16},{24,20},{28,24},{5,1},{9,5},{13... | collective-permute-start | bytes 6152 | tf_op jit(solution)/shard_map/ppermute | solution.py:27
  179.3 14.1 %collective-permute-start.10 = (bf16[16,64,1]{2,1,0:T(8,128)(2,1)S(1)}, bf16[16,64,1]{2,1,0:T(8,128)(2,1)S(1)}, u32[]{:S(2)}, u32[]{:S(2)}) collective-permute-start(bf16[16,64,1]{2,1,0:T(8,128)(2,1)S(1)} %get-tuple-element.16), channel_id=1, source_target_pairs={{0,4},{4,8},{8,12},{12,16},{16,20},{20,24},{24,28},{1,5},{5,9},{9,... | collective-permute-start | bytes 6152 | tf_op jit(solution)/shard_map/ppermute | solution.py:24
  186.0 7.4 %copy-start.6 = (f32[64,9,256]{2,0,1:T(8,128)}, f32[64,9,256]{2,0,1:T(8,128)S(1)}, u32[]{:S(2)}) copy-start(f32[64,9,256]{2,0,1:T(8,128)S(1)} %fusion.27) | copy-start | bytes 1769476
  194.1 1.0 copy-start.9
  198.9 109.5 %all-reduce.7.cloned.1.call-start = ((), (), s32[]{:S(2)}) async-start(), calls=%async_computation.4 | async-start | bytes 2359296 | tf_op jit(solution)/shard_map/psum | solution.py:96
  198.9 4.0 %copy-start.4 = (bf16[18,256,130]{2,1,0:T(8,128)(2,1)S(1)}, bf16[18,256,130]{2,1,0:T(8,128)(2,1)}, u32[]{:S(2)}) copy-start(bf16[18,256,130]{2,1,0:T(8,128)(2,1)} %maximum_select_fusion.2) | copy-start | bytes 3594244
  206.6 0.8 copy-start.7
Sparse Core Ops, SparseCore 0:
  150.5 26.1 reduce-scatter.2
  199.0 24.9 reduce-scatter.4
  228.1 80.2 all-reduce.6
